TPU v7x, 128 devices: a whole 4x4x4 slice. The times are simulated.
128 devices in a mesh: grp: 4 (over y), dev: 32 (over z, x, core).
Axes of the slice: x: 4, y: 4, z: 4, core: 2. Of those that a mesh axis runs over, the one named last changes fastest.
Arguments:
- points: float32 [64, 196608], P(None, 'dev'), may hold values from -6 to 6
- weights: float32 [196608, 128], P('dev'), may hold values from -4 to 4
- proj: float32 [256, 196608], P(None, 'dev'), may hold values from -0.078125 to 0.078125
- fetch_table: int32 [3, 32, 32, 2], P(None, 'dev'), may hold values from 0 to 11, as said below
- near_list: int32 [384, 16], P('dev'), may hold values from 0 to 63, as said below
- far_list: int32 [384, 8], P('dev'), may hold values from 0 to 31, as said below
- skel_idx: int32 [32, 256], P('dev'), may hold values from 0 to 6143, as said below
Outputs:
- potential: float32 [196608, 128], P('dev')
Inputs may be any that keep to these rules, and one draw needn't show every extreme that they name: Entries of fetch_table[r, d, e] are distinct local leaf numbers of column e. `near_list`: the 16 slots of one target leaf are distinct. `far_list`: the 8 nodes of one target leaf are distinct, and one of them is node (c + 1) mod 32 for the leaf's column c. `skel_idx`: the 256 skeleton points of one node are distinct.
All inputs are finite; a program needn't handle non-finite values.
Results may differ from a plain program's by a relative error of at most 0.0003.
Values sent between devices are 32-bit elements; how exact they have to be, the bound alone decides.
A program may use at most 192 MiB of HBM per device.

v0:
```python
import jax
import jax.numpy as jnp
from jax import lax
from jax.sharding import PartitionSpec as P


def kernel_sum(target, sources, values):
    high = lax.Precision.HIGHEST
    inner = jnp.einsum("dt,jds->tjs", target, sources, precision=high)
    target_norm = jnp.sum(target * target, axis=0)
    source_norm = jnp.sum(sources * sources, axis=1)
    distance = target_norm[:, None, None] + source_norm[None] - 2.0 * inner
    kernel = jnp.exp(-distance * (2.0 / target.shape[0]))
    return jnp.einsum("tjs,jsw->tw", kernel, values, precision=high)


def on_device(points, weights, proj, fetch_table, near_list, far_list, skel_idx):
    features, column_points = points.shape
    columns = weights.shape[1]
    devices = lax.axis_size("dev")
    groups = lax.axis_size("grp")
    targets = near_list.shape[0]
    leaf_size = column_points // targets
    row_leaves = targets // (groups - 1)
    capacity = fetch_table.shape[3]
    skeleton = skel_idx.shape[1]
    group_index = lax.axis_index("grp")
    near_row = jnp.minimum(group_index, groups - 2)
    far_side = group_index == groups - 1
    leaf_coords = points.reshape(features, targets, leaf_size)
    leaf_weights = weights.reshape(targets, leaf_size, columns)
    requests = lax.dynamic_index_in_dim(fetch_table[:, 0], near_row, 0, keepdims=False)
    asked = lax.all_to_all(requests, "dev", split_axis=0, concat_axis=0, tiled=True)
    coords = jnp.moveaxis(jnp.take(leaf_coords, asked, axis=1), 0, 2)
    values = jnp.take(leaf_weights, asked, axis=0)
    fetched_coords = lax.all_to_all(coords, "dev", split_axis=0, concat_axis=0, tiled=True)
    fetched_values = lax.all_to_all(values, "dev", split_axis=0, concat_axis=0, tiled=True)
    flat_coords = fetched_coords.reshape(devices * capacity, features, leaf_size)
    flat_values = fetched_values.reshape(devices * capacity, leaf_size, columns)
    local_skeleton = jnp.take(points, skel_idx[0], axis=1)
    share_len = column_points // groups
    share_start = group_index * share_len
    share_proj = lax.dynamic_slice_in_dim(proj, share_start, share_len, 1)
    share_weights = lax.dynamic_slice_in_dim(weights, share_start, share_len, 0)
    partial_value = jnp.dot(
        share_proj,
        share_weights,
        preferred_element_type=jnp.float32,
        precision=lax.Precision.HIGHEST,
    )
    node_index = lax.axis_index("dev")
    owner_mask = jnp.where(far_side, 1.0, 0.0).astype(jnp.float32)
    table_coords = jnp.zeros((devices, features, skeleton), jnp.float32)
    table_coords = lax.dynamic_update_index_in_dim(
        table_coords, local_skeleton * owner_mask, node_index, 0
    )
    table_weights = jnp.zeros((devices, skeleton, columns), jnp.float32)
    table_weights = lax.dynamic_update_index_in_dim(table_weights, partial_value, node_index, 0)
    skel_coords, skel_weights = lax.psum((table_coords, table_weights), ("grp", "dev"))

    def near_work():
        slots = lax.dynamic_slice_in_dim(near_list, near_row * row_leaves, row_leaves, 0)
        leaf_numbers = near_row * row_leaves + jnp.arange(row_leaves, dtype=jnp.int32)

        def near_leaf(items):
            leaf_number, leaf_slots = items
            target = jnp.take(leaf_coords, leaf_number, axis=1)
            return kernel_sum(
                target,
                jnp.take(flat_coords, leaf_slots, axis=0),
                jnp.take(flat_values, leaf_slots, axis=0),
            )

        block = lax.map(near_leaf, (leaf_numbers, slots))
        empty = jnp.zeros((targets, leaf_size, columns), jnp.float32)
        return lax.dynamic_update_slice_in_dim(empty, block, near_row * row_leaves, 0)

    def far_work():

        def far_leaf(items):
            leaf_number, node_ids = items
            target = jnp.take(leaf_coords, leaf_number, axis=1)
            return kernel_sum(
                target,
                jnp.take(skel_coords, node_ids, axis=0),
                jnp.take(skel_weights, node_ids, axis=0),
            )

        return lax.map(far_leaf, (jnp.arange(targets, dtype=jnp.int32), far_list))

    contribution = lax.cond(far_side, far_work, near_work)
    total = lax.psum(contribution, "grp")
    return total.reshape(column_points, columns)


def solution(mesh):
    placed = (
        P(None, "dev"),
        P("dev", None),
        P(None, "dev"),
        P(None, "dev", None, None),
        P("dev", None),
        P("dev", None),
        P("dev", None),
    )
    return jax.shard_map(
        on_device, mesh=mesh, in_specs=placed, out_specs=P("dev", None), check_vma=False
    )
```

profile of v0, /device:TPU:1, one launch (start us, length us, event | category | flops | bytes accessed | tf_op | source)
XLA Modules:
  0.0 820.4 jit_solution(13350892789192930071)
XLA Ops:
  8.1 9.4 %all-to-all-start = ((s32[32,1,2]{2,1,0:T(1,128)}), s32[32,1,2]{2,1,0:T(1,128)S(1)}, u32[]{:S(2)}, u32[]{:S(2)}) async-start(s32[32,1,2]{2,1,0:T(1,128)} %copy.36), calls=%async_computation | async-start | bytes 32768 | tf_op jit(solution)/shard_map/all_to_all | solution.py:33
  24.8 5.7 gather_fusion.4
  30.6 8.5 %broadcast_select_fusion.1 = f32[32,2,64,512]{3,2,1,0:T(8,128)} fusion(f32[32,2,64,512]{3,2,1,0:T(8,128)} %bitcast.103, pred[32,2]{1,0:T(8,128)(4,1)S(1)} %copy.38), kind=kLoop, calls=%fused_computation.87 | loop fusion | flops 2097152 | bytes 16777280 | tf_op jit(solution)/shard_map/jit(_take)/select_n | solution.py:34
  39.1 5.2 all-to-all-start.1
  44.3 7.4 gather_fusion.5
  51.6 11.6 %broadcast_select_fusion = f32[32,2,512,128]{3,2,1,0:T(8,128)} fusion(f32[32,2,512,128]{3,2,1,0:T(8,128)} %bitcast.101, pred[32,2]{1,0:T(8,128)(4,1)S(1)} %copy.38), kind=kLoop, calls=%fused_computation.86 | loop fusion | flops 4194304 | bytes 33554496 | tf_op jit(solution)/shard_map/jit(_take)/select_n | solution.py:35
  63.2 80.8 %all-to-all-done.1 = f32[32,2,64,512]{3,2,1,0:T(8,128)} async-done(((f32[32,2,64,512]{3,2,1,0:T(8,128)}), f32[32,2,64,512]{3,2,1,0:T(8,128)}, u32[]{:S(2)}, u32[]{:S(2)}) %all-to-all-start.1) | async-done | bytes 8388640 | tf_op jit(solution)/shard_map/all_to_all | solution.py:36
  144.0 11.3 %all-to-all-start.2 = ((f32[32,2,512,128]{3,2,1,0:T(8,128)}), f32[32,2,512,128]{3,2,1,0:T(8,128)}, u32[]{:S(2)}, u32[]{:S(2)}) async-start(f32[32,2,512,128]{3,2,1,0:T(8,128)} %broadcast_select_fusion), calls=%async_computation.2 | async-start | bytes 33554432 | tf_op jit(solution)/shard_map/all_to_all | solution.py:37
  171.4 310.3 %all-reduce.6.cloned.1.call-done = (f32[32,64,256]{2,1,0:T(8,128)}, f32[32,256,128]{2,1,0:T(8,128)}) async-done(((f32[32,64,256]{2,1,0:T(8,128)}, f32[32,256,128]{2,1,0:T(8,128)}), (f32[32,64,256]{2,1,0:T(8,128)}, f32[32,256,128]{2,1,0:T(8,128)})) %all-reduce.6.cloned.1.call-update) | async-done | bytes 6291472 | tf_op jit(solution)/shard_map/psum | solution.py:59
  481.8 223.2 %conditional.1 = (f32[12,512,128]{2,1,0:T(8,128)}) conditional(s32[]{:T(128)} %convert_element_type.3, (s32[]{:T(128)}, s32[12,16]{1,0:T(8,128)}, f32[32,2,64,512]{3,2,1,0:T(8,128)}, f32[32,2,512,128]{3,2,1,0:T(8,128)}, f32[64,12,512]{2,1,0:T(8,128)}) %tuple.20, (f32[64,12,512]{2,1,0:T(8,128)}, s32[12,8]{0,1:T(8,128)S(1)}, f32[32,64,256]{2,1,0:T(8,128)}, ...), branch_computations={%region_2.0_spmd, %region_7.13_spmd} | conditional | flops 9687917568 | bytes 60630836 | solution.py:91
  482.4 218.3 %while.19 = (s32[]{:T(128)}, f32[4,512,128]{2,1,0:T(8,128)}, s32[4]{0:T(128)S(1)}, f32[64,12,512]{2,1,0:T(8,128)}, s32[4,16]{1,0:T(4,128)S(1)}, /*index=5*/f32[6...) while((s32[]{:T(128)}, f32[4,512,128]{2,1,0:T(8,128)}, ...), condition=%wide.region_6.7_spmd, body=%wide.region_3.6_spmd.sunk | while | flops 9687917568 | bytes 55387260 | solution.py:74
  490.4 16.2 %fusion.112 = f32[512,16,512]{2,0,1:T(8,128)} fusion(f32[16,64,512]{2,1,0:T(8,128)S(1)} %gather_fusion.3, pred[16]{0:T(512)(128)(4,1)S(1)} %compare_and_fusion.7, f32[64,1,512]{2,1,0:T(1,128)S(1)} %constant_dynamic-slice_fusion.9, pred[]{:T(512)S(6)} %and.57), kind=kOutput, calls=%fused_computation.22.clone.1 | convolution fusion | flops 3221782528 | bytes 19005456 | tf_op jit(solution)/shard_map/cond/branch_0_fun/while/body/eval_jaxpr/dt,jds->tjs/dot_general | solution.py:9
  507.0 8.5 %gather_fusion.2 = f32[16,512,128]{2,1,0:T(8,128)} fusion(f32[64,512,128]{2,1,0:T(8,128)} %get-tuple-element.330, s32[1024]{0:T(1024)S(1)} %pad_clamp_fusion.7), kind=kCustom, calls=%fused_computation.1.clone.1 | custom fusion | bytes 8388672 | tf_op jit(solution)/shard_map/cond/branch_0_fun/while/body/eval_jaxpr/jit(_take)/gather | solution.py:71
  515.5 21.5 %fusion.114 = f32[4,512,128]{2,1,0:T(8,128)} fusion(f32[4,512,128]{2,1,0:T(8,128)} %get-tuple-element.314, s32[]{:T(128)} %get-tuple-element.313, f32[16,512,128]{2,1,0:T(8,128)} %gather_fusion.2, pred[16]{0:T(512)(128)(4,1)S(1)} %compare_and_fusion.7, f32[512,16,512]{2,0,1:T(8,128)} %fusion.112, f32[16,512]{1,0:T(8,128)S(1)} %multiply_reduce_fusion.5, ...), kind=kOutput, calls=%fused_computation.25.clone.1 | convolution fusion | flops 6464471040 | bytes 21269008 | tf_op jit(solution)/shard_map/cond/branch_0_fun/while/body/eval_jaxpr/tjs,jsw->tw/dot_general | solution.py:14
  545.0 16.2 %fusion.112 = f32[512,16,512]{2,0,1:T(8,128)} fusion(f32[16,64,512]{2,1,0:T(8,128)S(1)} %gather_fusion.3, pred[16]{0:T(512)(128)(4,1)S(1)} %compare_and_fusion.7, f32[64,1,512]{2,1,0:T(1,128)S(1)} %constant_dynamic-slice_fusion.9, pred[]{:T(512)S(6)} %and.57), kind=kOutput, calls=%fused_computation.22.clone.1 | convolution fusion | flops 3221782528 | bytes 19005456 | tf_op jit(solution)/shard_map/cond/branch_0_fun/while/body/eval_jaxpr/dt,jds->tjs/dot_general | solution.py:9
  561.5 8.5 %gather_fusion.2 = f32[16,512,128]{2,1,0:T(8,128)} fusion(f32[64,512,128]{2,1,0:T(8,128)} %get-tuple-element.330, s32[1024]{0:T(1024)S(1)} %pad_clamp_fusion.7), kind=kCustom, calls=%fused_computation.1.clone.1 | custom fusion | bytes 8388672 | tf_op jit(solution)/shard_map/cond/branch_0_fun/while/body/eval_jaxpr/jit(_take)/gather | solution.py:71
  570.1 21.5 %fusion.114 = f32[4,512,128]{2,1,0:T(8,128)} fusion(f32[4,512,128]{2,1,0:T(8,128)} %get-tuple-element.314, s32[]{:T(128)} %get-tuple-element.313, f32[16,512,128]{2,1,0:T(8,128)} %gather_fusion.2, pred[16]{0:T(512)(128)(4,1)S(1)} %compare_and_fusion.7, f32[512,16,512]{2,0,1:T(8,128)} %fusion.112, f32[16,512]{1,0:T(8,128)S(1)} %multiply_reduce_fusion.5, ...), kind=kOutput, calls=%fused_computation.25.clone.1 | convolution fusion | flops 6464471040 | bytes 21269008 | tf_op jit(solution)/shard_map/cond/branch_0_fun/while/body/eval_jaxpr/tjs,jsw->tw/dot_general | solution.py:14
  599.5 16.2 %fusion.112 = f32[512,16,512]{2,0,1:T(8,128)} fusion(f32[16,64,512]{2,1,0:T(8,128)S(1)} %gather_fusion.3, pred[16]{0:T(512)(128)(4,1)S(1)} %compare_and_fusion.7, f32[64,1,512]{2,1,0:T(1,128)S(1)} %constant_dynamic-slice_fusion.9, pred[]{:T(512)S(6)} %and.57), kind=kOutput, calls=%fused_computation.22.clone.1 | convolution fusion | flops 3221782528 | bytes 19005456 | tf_op jit(solution)/shard_map/cond/branch_0_fun/while/body/eval_jaxpr/dt,jds->tjs/dot_general | solution.py:9
  616.1 8.5 %gather_fusion.2 = f32[16,512,128]{2,1,0:T(8,128)} fusion(f32[64,512,128]{2,1,0:T(8,128)} %get-tuple-element.330, s32[1024]{0:T(1024)S(1)} %pad_clamp_fusion.7), kind=kCustom, calls=%fused_computation.1.clone.1 | custom fusion | bytes 8388672 | tf_op jit(solution)/shard_map/cond/branch_0_fun/while/body/eval_jaxpr/jit(_take)/gather | solution.py:71
  624.6 21.5 %fusion.114 = f32[4,512,128]{2,1,0:T(8,128)} fusion(f32[4,512,128]{2,1,0:T(8,128)} %get-tuple-element.314, s32[]{:T(128)} %get-tuple-element.313, f32[16,512,128]{2,1,0:T(8,128)} %gather_fusion.2, pred[16]{0:T(512)(128)(4,1)S(1)} %compare_and_fusion.7, f32[512,16,512]{2,0,1:T(8,128)} %fusion.112, f32[16,512]{1,0:T(8,128)S(1)} %multiply_reduce_fusion.5, ...), kind=kOutput, calls=%fused_computation.25.clone.1 | convolution fusion | flops 6464471040 | bytes 21269008 | tf_op jit(solution)/shard_map/cond/branch_0_fun/while/body/eval_jaxpr/tjs,jsw->tw/dot_general | solution.py:14
  654.1 16.2 %fusion.112 = f32[512,16,512]{2,0,1:T(8,128)} fusion(f32[16,64,512]{2,1,0:T(8,128)S(1)} %gather_fusion.3, pred[16]{0:T(512)(128)(4,1)S(1)} %compare_and_fusion.7, f32[64,1,512]{2,1,0:T(1,128)S(1)} %constant_dynamic-slice_fusion.9, pred[]{:T(512)S(6)} %and.57), kind=kOutput, calls=%fused_computation.22.clone.1 | convolution fusion | flops 3221782528 | bytes 19005456 | tf_op jit(solution)/shard_map/cond/branch_0_fun/while/body/eval_jaxpr/dt,jds->tjs/dot_general | solution.py:9
  670.7 8.5 %gather_fusion.2 = f32[16,512,128]{2,1,0:T(8,128)} fusion(f32[64,512,128]{2,1,0:T(8,128)} %get-tuple-element.330, s32[1024]{0:T(1024)S(1)} %pad_clamp_fusion.7), kind=kCustom, calls=%fused_computation.1.clone.1 | custom fusion | bytes 8388672 | tf_op jit(solution)/shard_map/cond/branch_0_fun/while/body/eval_jaxpr/jit(_take)/gather | solution.py:71
  679.2 21.5 %fusion.114 = f32[4,512,128]{2,1,0:T(8,128)} fusion(f32[4,512,128]{2,1,0:T(8,128)} %get-tuple-element.314, s32[]{:T(128)} %get-tuple-element.313, f32[16,512,128]{2,1,0:T(8,128)} %gather_fusion.2, pred[16]{0:T(512)(128)(4,1)S(1)} %compare_and_fusion.7, f32[512,16,512]{2,0,1:T(8,128)} %fusion.112, f32[16,512]{1,0:T(8,128)S(1)} %multiply_reduce_fusion.5, ...), kind=kOutput, calls=%fused_computation.25.clone.1 | convolution fusion | flops 6464471040 | bytes 21269008 | tf_op jit(solution)/shard_map/cond/branch_0_fun/while/body/eval_jaxpr/tjs,jsw->tw/dot_general | solution.py:14
  705.0 104.8 %all-reduce.4.cloned.1.call-done = f32[6144,128]{1,0:T(8,128)} async-done(((f32[6144,128]{1,0:T(8,128)}), f32[6144,128]{1,0:T(8,128)}) %all-reduce.4.cloned.1.call-update) | async-done | bytes 3145744 | tf_op jit(solution)/shard_map/psum | solution.py:92
  (75 shorter events, 59.4 us)
Async XLA Ops:
  6.5 37.7 %copy-start = (f32[6144,128]{1,0:T(8,128)S(1)}, f32[6144,128]{1,0:T(8,128)}, u32[]{:S(2)}) copy-start(f32[6144,128]{1,0:T(8,128)} %param.16) | copy-start | bytes 9437188
  8.1 16.4 %all-to-all-start = ((s32[32,1,2]{2,1,0:T(1,128)}), s32[32,1,2]{2,1,0:T(1,128)S(1)}, u32[]{:S(2)}, u32[]{:S(2)}) async-start(s32[32,1,2]{2,1,0:T(1,128)} %copy.36), calls=%async_computation | async-start | bytes 32768 | tf_op jit(solution)/shard_map/all_to_all | solution.py:33
  39.1 105.0 %all-to-all-start.1 = ((f32[32,2,64,512]{3,2,1,0:T(8,128)}), f32[32,2,64,512]{3,2,1,0:T(8,128)}, u32[]{:S(2)}, u32[]{:S(2)}) async-start(f32[32,2,64,512]{3,2,1,0:T(8,128)} %broadcast_select_fusion.1), calls=%async_computation.1 | async-start | bytes 16777216 | tf_op jit(solution)/shard_map/all_to_all | solution.py:36
  144.0 337.7 %all-to-all-start.2 = ((f32[32,2,512,128]{3,2,1,0:T(8,128)}), f32[32,2,512,128]{3,2,1,0:T(8,128)}, u32[]{:S(2)}, u32[]{:S(2)}) async-start(f32[32,2,512,128]{3,2,1,0:T(8,128)} %broadcast_select_fusion), calls=%async_computation.2 | async-start | bytes 33554432 | tf_op jit(solution)/shard_map/all_to_all | solution.py:37
  155.3 3.3 copy-start.4
  155.3 326.4 %all-reduce.6.cloned.1.call-start = ((), (), s32[]{:S(2)}) async-start(), calls=%async_computation.4 | async-start | bytes 12582912 | tf_op jit(solution)/shard_map/psum | solution.py:59
  167.2 2.3 copy-start.2
  169.4 312.3 %copy-start.3 = (s32[12,8]{0,1:T(8,128)S(1)}, s32[12,8]{0,1:T(8,128)}, u32[]{:S(2)}) copy-start(s32[12,8]{0,1:T(8,128)} %param.20) | copy-start | bytes 1156
  169.5 640.3 %all-reduce.4.cloned.1.call-start = ((), (), s32[]{:S(2)}) async-start(), calls=%async_computation.3 | async-start | bytes 6291456 | tf_op jit(solution)/shard_map/psum | solution.py:92
  705.0 108.6 %copy-start.1 = (f32[6144,128]{1,0:T(8,128)S(1)}, f32[6144,128]{1,0:T(8,128)}, u32[]{:S(2)}) copy-start(f32[6144,128]{1,0:T(8,128)} %param.16) | copy-start | bytes 9437188
Sparse Core Ops, SparseCore 0:
  169.6 312.1 all-reduce.5
  705.1 104.6 all-reduce.3
where the time goes:
time: 823 us; the launch traced here: 820 us
  waiting for transfers between devices  500 us (61%)
  matrix products  154 us (19%)
  local copies, waits for them, and re-layouts  96.2 us (12%)
  starting transfers between devices  26 us (3%)
  other arithmetic  22.5 us (3%)
  between operations  13.5 us (2%)
    psum x1, waiting for transfers between devices, on_device(): lax.psum((table_coords, table_weights), ('grp', 'dev'))  310 us
    psum x1, waiting for transfers between devices, on_device(): total = lax.psum(contribution, 'grp')  105 us
    dot_general x4, matrix products, kernel_sum(): return jnp.einsum('tjs,jsw->tw', kernel, values, precision=high)  86.1 us
    all_to_all x1, waiting for transfers between devices, on_device(): lax.all_to_all(coords, 'dev', split_axis=0, concat_axis=0, tiled=True)  80.8 us
    dot_general x4, matrix products, kernel_sum(): inner = jnp.einsum('dt,jds->tjs', target, sources, precision=high)  64.7 us
    gather x4, local copies, waits for them, and re-layouts, near_leaf(): jnp.take(flat_values, leaf_slots, axis=0)  34 us
  transfers between devices with their start and end apart: 5, of which 4 were waited for; matrix products, arithmetic and copies ran while one was open for 5% of the time, Pallas kernels for 0%

commit v1 on v0

--- a/solution.py
+++ b/solution.py
@@ -89,7 +89,9 @@
         return lax.map(far_leaf, (jnp.arange(targets, dtype=jnp.int32), far_list))
 
     contribution = lax.cond(far_side, far_work, near_work)
-    total = lax.psum(contribution, "grp")
+    total = contribution
+    for hop in (1, 2):
+        total = total + lax.ppermute(total, "grp", [(dev, dev ^ hop) for dev in range(4)])
     return total.reshape(column_points, columns)
 
 

time: 823 us -> 889 us (1.080)
  starting transfers between devices: 26 us -> 59.9 us
  waiting for transfers between devices: 500 us -> 531 us
    ppermute x0 -> x2, waiting for transfers between devices: none -> 136 us  [on_device(): lax.ppermute(total, 'grp', [(dev, dev ^ hop) for dev in range(4)])]
    psum x1 -> x0, waiting for transfers between devices: 105 us -> none  [on_device(): total = lax.psum(contribution, 'grp')]
    ppermute x0 -> x2, starting transfers between devices: none -> 34 us  [on_device(): lax.ppermute(total, 'grp', [(dev, dev ^ hop) for dev in range(4)])]
  transfers between devices with their start and end apart: 5 -> 6, of which waited for: 4 -> 5; matrix products, arithmetic and copies ran while one was open for 5% -> 4% of each run, Pallas kernels for 0% -> 0%
where the time goes in v1:
time: 889 us; the launch traced here: 886 us
  waiting for transfers between devices  531 us (60%)
  matrix products  154 us (17%)
  local copies, waits for them, and re-layouts  92.6 us (10%)
  starting transfers between devices  59.9 us (7%)
  other arithmetic  26.9 us (3%)
  between operations  13.5 us (2%)
    psum x1, waiting for transfers between devices, on_device(): lax.psum((table_coords, table_weights), ('grp', 'dev'))  310 us
    ppermute x2, waiting for transfers between devices, on_device(): lax.ppermute(total, 'grp', [(dev, dev ^ hop) for dev in range(4)])  136 us
    dot_general x4, matrix products, kernel_sum(): return jnp.einsum('tjs,jsw->tw', kernel, values, precision=high)  86.1 us
    all_to_all x1, waiting for transfers between devices, on_device(): lax.all_to_all(coords, 'dev', split_axis=0, concat_axis=0, tiled=True)  80.8 us
    dot_general x4, matrix products, kernel_sum(): inner = jnp.einsum('dt,jds->tjs', target, sources, precision=high)  64.7 us
    gather x4, local copies, waits for them, and re-layouts, near_leaf(): jnp.take(flat_values, leaf_slots, axis=0)  34.1 us
    ppermute x2, starting transfers between devices, on_device(): lax.ppermute(total, 'grp', [(dev, dev ^ hop) for dev in range(4)])  34 us
  transfers between devices with their start and end apart: 6, of which 5 were waited for; matrix products, arithmetic and copies ran while one was open for 4% of the time, Pallas kernels for 0%

profile of v1, /device:TPU:1, one launch (start us, length us, event | category | flops | bytes accessed | tf_op | source)
XLA Modules:
  0.0 886.0 jit_solution(14570256411005428466)
XLA Ops:
  8.1 9.4 %all-to-all-start = ((s32[32,1,2]{2,1,0:T(1,128)}), s32[32,1,2]{2,1,0:T(1,128)S(1)}, u32[]{:S(2)}, u32[]{:S(2)}) async-start(s32[32,1,2]{2,1,0:T(1,128)} %copy.36), calls=%async_computation | async-start | bytes 32768 | tf_op jit(solution)/shard_map/all_to_all | solution.py:33
  30.6 8.5 broadcast_select_fusion.1
  44.3 7.4 gather_fusion.5
  51.6 11.6 %broadcast_select_fusion = f32[32,2,512,128]{3,2,1,0:T(8,128)} fusion(f32[32,2,512,128]{3,2,1,0:T(8,128)} %bitcast.101, pred[32,2]{1,0:T(8,128)(4,1)S(1)} %copy.38), kind=kLoop, calls=%fused_computation.86 | loop fusion | flops 4194304 | bytes 33554496 | tf_op jit(solution)/shard_map/jit(_take)/select_n | solution.py:35
  63.2 80.8 %all-to-all-done.1 = f32[32,2,64,512]{3,2,1,0:T(8,128)} async-done(((f32[32,2,64,512]{3,2,1,0:T(8,128)}), f32[32,2,64,512]{3,2,1,0:T(8,128)}, u32[]{:S(2)}, u32[]{:S(2)}) %all-to-all-start.1) | async-done | bytes 8388640 | tf_op jit(solution)/shard_map/all_to_all | solution.py:36
  144.0 11.3 %all-to-all-start.2 = ((f32[32,2,512,128]{3,2,1,0:T(8,128)}), f32[32,2,512,128]{3,2,1,0:T(8,128)}, u32[]{:S(2)}, u32[]{:S(2)}) async-start(f32[32,2,512,128]{3,2,1,0:T(8,128)} %broadcast_select_fusion), calls=%async_computation.2 | async-start | bytes 33554432 | tf_op jit(solution)/shard_map/all_to_all | solution.py:37
  171.4 310.4 %all-reduce.3.cloned.1.call-done = (f32[32,64,256]{2,1,0:T(8,128)}, f32[32,256,128]{2,1,0:T(8,128)}) async-done(((f32[32,64,256]{2,1,0:T(8,128)}, f32[32,256,128]{2,1,0:T(8,128)}), (f32[32,64,256]{2,1,0:T(8,128)}, f32[32,256,128]{2,1,0:T(8,128)})) %all-reduce.3.cloned.1.call-update) | async-done | bytes 6291472 | tf_op jit(solution)/shard_map/psum | solution.py:59
  481.8 223.1 %conditional.1 = (f32[12,512,128]{2,1,0:T(8,128)}) conditional(s32[]{:T(128)} %convert_element_type.3, (s32[]{:T(128)}, s32[12,16]{1,0:T(8,128)}, f32[32,2,64,512]{3,2,1,0:T(8,128)}, f32[32,2,512,128]{3,2,1,0:T(8,128)}, f32[64,12,512]{2,1,0:T(8,128)}) %tuple.20, (f32[64,12,512]{2,1,0:T(8,128)}, s32[12,8]{0,1:T(8,128)S(1)}, f32[32,64,256]{2,1,0:T(8,128)}, ...), branch_computations={%region_2.0_spmd, %region_7.13_spmd} | conditional | flops 9687917568 | bytes 60630836 | solution.py:91
  482.5 218.2 %while.19 = (s32[]{:T(128)}, f32[4,512,128]{2,1,0:T(8,128)}, s32[4]{0:T(128)S(1)}, f32[64,12,512]{2,1,0:T(8,128)}, s32[4,16]{1,0:T(4,128)S(1)}, /*index=5*/f32[6...) while((s32[]{:T(128)}, f32[4,512,128]{2,1,0:T(8,128)}, ...), condition=%wide.region_6.7_spmd, body=%wide.region_3.6_spmd.sunk | while | flops 9687917568 | bytes 55387260 | solution.py:74
  490.4 16.2 %fusion.112 = f32[512,16,512]{2,0,1:T(8,128)} fusion(f32[16,64,512]{2,1,0:T(8,128)S(1)} %gather_fusion.3, pred[16]{0:T(512)(128)(4,1)S(1)} %compare_and_fusion.7, f32[64,1,512]{2,1,0:T(1,128)S(1)} %constant_dynamic-slice_fusion.9, pred[]{:T(512)S(6)} %and.57), kind=kOutput, calls=%fused_computation.22.clone.1 | convolution fusion | flops 3221782528 | bytes 19005456 | tf_op jit(solution)/shard_map/cond/branch_0_fun/while/body/eval_jaxpr/dt,jds->tjs/dot_general | solution.py:9
  507.0 8.5 gather_fusion.2
  515.5 21.5 %fusion.114 = f32[4,512,128]{2,1,0:T(8,128)} fusion(f32[4,512,128]{2,1,0:T(8,128)} %get-tuple-element.314, s32[]{:T(128)} %get-tuple-element.313, f32[16,512,128]{2,1,0:T(8,128)} %gather_fusion.2, pred[16]{0:T(512)(128)(4,1)S(1)} %compare_and_fusion.7, f32[512,16,512]{2,0,1:T(8,128)} %fusion.112, f32[16,512]{1,0:T(8,128)S(1)} %multiply_reduce_fusion.5, ...), kind=kOutput, calls=%fused_computation.25.clone.1 | convolution fusion | flops 6464471040 | bytes 21269008 | tf_op jit(solution)/shard_map/cond/branch_0_fun/while/body/eval_jaxpr/tjs,jsw->tw/dot_general | solution.py:14
  545.0 16.2 %fusion.112 = f32[512,16,512]{2,0,1:T(8,128)} fusion(f32[16,64,512]{2,1,0:T(8,128)S(1)} %gather_fusion.3, pred[16]{0:T(512)(128)(4,1)S(1)} %compare_and_fusion.7, f32[64,1,512]{2,1,0:T(1,128)S(1)} %constant_dynamic-slice_fusion.9, pred[]{:T(512)S(6)} %and.57), kind=kOutput, calls=%fused_computation.22.clone.1 | convolution fusion | flops 3221782528 | bytes 19005456 | tf_op jit(solution)/shard_map/cond/branch_0_fun/while/body/eval_jaxpr/dt,jds->tjs/dot_general | solution.py:9
  561.6 8.5 gather_fusion.2
  570.1 21.5 %fusion.114 = f32[4,512,128]{2,1,0:T(8,128)} fusion(f32[4,512,128]{2,1,0:T(8,128)} %get-tuple-element.314, s32[]{:T(128)} %get-tuple-element.313, f32[16,512,128]{2,1,0:T(8,128)} %gather_fusion.2, pred[16]{0:T(512)(128)(4,1)S(1)} %compare_and_fusion.7, f32[512,16,512]{2,0,1:T(8,128)} %fusion.112, f32[16,512]{1,0:T(8,128)S(1)} %multiply_reduce_fusion.5, ...), kind=kOutput, calls=%fused_computation.25.clone.1 | convolution fusion | flops 6464471040 | bytes 21269008 | tf_op jit(solution)/shard_map/cond/branch_0_fun/while/body/eval_jaxpr/tjs,jsw->tw/dot_general | solution.py:14
  599.5 16.2 %fusion.112 = f32[512,16,512]{2,0,1:T(8,128)} fusion(f32[16,64,512]{2,1,0:T(8,128)S(1)} %gather_fusion.3, pred[16]{0:T(512)(128)(4,1)S(1)} %compare_and_fusion.7, f32[64,1,512]{2,1,0:T(1,128)S(1)} %constant_dynamic-slice_fusion.9, pred[]{:T(512)S(6)} %and.57), kind=kOutput, calls=%fused_computation.22.clone.1 | convolution fusion | flops 3221782528 | bytes 19005456 | tf_op jit(solution)/shard_map/cond/branch_0_fun/while/body/eval_jaxpr/dt,jds->tjs/dot_general | solution.py:9
  616.1 8.5 gather_fusion.2
  624.6 21.5 %fusion.114 = f32[4,512,128]{2,1,0:T(8,128)} fusion(f32[4,512,128]{2,1,0:T(8,128)} %get-tuple-element.314, s32[]{:T(128)} %get-tuple-element.313, f32[16,512,128]{2,1,0:T(8,128)} %gather_fusion.2, pred[16]{0:T(512)(128)(4,1)S(1)} %compare_and_fusion.7, f32[512,16,512]{2,0,1:T(8,128)} %fusion.112, f32[16,512]{1,0:T(8,128)S(1)} %multiply_reduce_fusion.5, ...), kind=kOutput, calls=%fused_computation.25.clone.1 | convolution fusion | flops 6464471040 | bytes 21269008 | tf_op jit(solution)/shard_map/cond/branch_0_fun/while/body/eval_jaxpr/tjs,jsw->tw/dot_general | solution.py:14
  654.1 16.2 %fusion.112 = f32[512,16,512]{2,0,1:T(8,128)} fusion(f32[16,64,512]{2,1,0:T(8,128)S(1)} %gather_fusion.3, pred[16]{0:T(512)(128)(4,1)S(1)} %compare_and_fusion.7, f32[64,1,512]{2,1,0:T(1,128)S(1)} %constant_dynamic-slice_fusion.9, pred[]{:T(512)S(6)} %and.57), kind=kOutput, calls=%fused_computation.22.clone.1 | convolution fusion | flops 3221782528 | bytes 19005456 | tf_op jit(solution)/shard_map/cond/branch_0_fun/while/body/eval_jaxpr/dt,jds->tjs/dot_general | solution.py:9
  670.7 8.5 gather_fusion.2
  679.2 21.5 %fusion.114 = f32[4,512,128]{2,1,0:T(8,128)} fusion(f32[4,512,128]{2,1,0:T(8,128)} %get-tuple-element.314, s32[]{:T(128)} %get-tuple-element.313, f32[16,512,128]{2,1,0:T(8,128)} %gather_fusion.2, pred[16]{0:T(512)(128)(4,1)S(1)} %compare_and_fusion.7, f32[512,16,512]{2,0,1:T(8,128)} %fusion.112, f32[16,512]{1,0:T(8,128)S(1)} %multiply_reduce_fusion.5, ...), kind=kOutput, calls=%fused_computation.25.clone.1 | convolution fusion | flops 6464471040 | bytes 21269008 | tf_op jit(solution)/shard_map/cond/branch_0_fun/while/body/eval_jaxpr/tjs,jsw->tw/dot_general | solution.py:14
  705.4 68.3 %collective-permute-done = f32[12,512,128]{2,1,0:T(8,128)S(1)} collective-permute-done((f32[12,512,128]{2,1,0:T(8,128)}, f32[12,512,128]{2,1,0:T(8,128)S(1)}, u32[]{:S(2)}, u32[]{:S(2)}) %collective-permute-start) | collective-permute-done | bytes 3145760 | tf_op jit(solution)/shard_map/ppermute | solution.py:94
  776.0 33.6 %collective-permute-start.1 = (f32[12,512,128]{2,1,0:T(8,128)S(1)}, f32[12,512,128]{2,1,0:T(8,128)S(1)}, u32[]{:S(2)}, u32[]{:S(2)}) collective-permute-start(f32[12,512,128]{2,1,0:T(8,128)S(1)} %add.160), channel_id=1, source_target_pairs={{0,64},{32,96},{64,0},{96,32},{1,65},{33,97},{65,1},{97,33},{2,66}... | collective-permute-start | bytes 9437192 | tf_op jit(solution)/shard_map/ppermute | solution.py:94
  809.6 67.6 %collective-permute-done.1 = f32[12,512,128]{2,1,0:T(8,128)S(1)} collective-permute-done((f32[12,512,128]{2,1,0:T(8,128)S(1)}, f32[12,512,128]{2,1,0:T(8,128)S(1)}, u32[]{:S(2)}, u32[]{:S(2)}) %collective-permute-start.1) | collective-permute-done | bytes 3145760 | tf_op jit(solution)/shard_map/ppermute | solution.py:94
  (77 shorter events, 71.3 us)
Async XLA Ops:
  6.5 37.7 %copy-start = (f32[6144,128]{1,0:T(8,128)S(1)}, f32[6144,128]{1,0:T(8,128)}, u32[]{:S(2)}) copy-start(f32[6144,128]{1,0:T(8,128)} %param.16) | copy-start | bytes 9437188
  8.1 16.4 %all-to-all-start = ((s32[32,1,2]{2,1,0:T(1,128)}), s32[32,1,2]{2,1,0:T(1,128)S(1)}, u32[]{:S(2)}, u32[]{:S(2)}) async-start(s32[32,1,2]{2,1,0:T(1,128)} %copy.36), calls=%async_computation | async-start | bytes 32768 | tf_op jit(solution)/shard_map/all_to_all | solution.py:33
  39.1 105.0 %all-to-all-start.1 = ((f32[32,2,64,512]{3,2,1,0:T(8,128)}), f32[32,2,64,512]{3,2,1,0:T(8,128)}, u32[]{:S(2)}, u32[]{:S(2)}) async-start(f32[32,2,64,512]{3,2,1,0:T(8,128)} %broadcast_select_fusion.1), calls=%async_computation.1 | async-start | bytes 16777216 | tf_op jit(solution)/shard_map/all_to_all | solution.py:36
  144.0 337.8 %all-to-all-start.2 = ((f32[32,2,512,128]{3,2,1,0:T(8,128)}), f32[32,2,512,128]{3,2,1,0:T(8,128)}, u32[]{:S(2)}, u32[]{:S(2)}) async-start(f32[32,2,512,128]{3,2,1,0:T(8,128)} %broadcast_select_fusion), calls=%async_computation.2 | async-start | bytes 33554432 | tf_op jit(solution)/shard_map/all_to_all | solution.py:37
  155.3 3.3 copy-start.4
  155.3 326.5 %all-reduce.3.cloned.1.call-start = ((), (), s32[]{:S(2)}) async-start(), calls=%async_computation.3 | async-start | bytes 12582912 | tf_op jit(solution)/shard_map/psum | solution.py:59
  167.3 2.2 copy-start.2
  169.5 312.3 %copy-start.3 = (s32[12,8]{0,1:T(8,128)S(1)}, s32[12,8]{0,1:T(8,128)}, u32[]{:S(2)}) copy-start(s32[12,8]{0,1:T(8,128)} %param.20) | copy-start | bytes 1156
  705.0 68.7 %collective-permute-start = (f32[12,512,128]{2,1,0:T(8,128)}, f32[12,512,128]{2,1,0:T(8,128)S(1)}, u32[]{:S(2)}, u32[]{:S(2)}) collective-permute-start(f32[12,512,128]{2,1,0:T(8,128)} %get-tuple-element.337), channel_id=1, source_target_pairs={{0,32},{32,0},{64,96},{96,64},{1,33},{33,1},{65,97},{97,65},{2,34}... | collective-permute-start | bytes 9437192 | tf_op jit(solution)/shard_map/ppermute | solution.py:94
  773.7 105.5 %copy-start.1 = (f32[6144,128]{1,0:T(8,128)S(1)}, f32[6144,128]{1,0:T(8,128)}, u32[]{:S(2)}) copy-start(f32[6144,128]{1,0:T(8,128)} %param.16) | copy-start | bytes 9437188
  776.0 101.2 %collective-permute-start.1 = (f32[12,512,128]{2,1,0:T(8,128)S(1)}, f32[12,512,128]{2,1,0:T(8,128)S(1)}, u32[]{:S(2)}, u32[]{:S(2)}) collective-permute-start(f32[12,512,128]{2,1,0:T(8,128)S(1)} %add.160), channel_id=1, source_target_pairs={{0,64},{32,96},{64,0},{96,32},{1,65},{33,97},{65,1},{97,33},{2,66}... | collective-permute-start | bytes 9437192 | tf_op jit(solution)/shard_map/ppermute | solution.py:94
Sparse Core Ops, SparseCore 0:
  169.6 312.1 all-reduce.2
